TPU v7x, 256 devices: a whole 4x4x8 slice. The times are simulated.
256 devices in a mesh: dom: 32 (over z, y_hi, core), orb: 8 (over y_lo, x).
Axes of the slice: x: 4, y: 4 (y_hi: 2, y_lo: 2; y = y_hi * 2 + y_lo), z: 8, core: 2. Of those that a mesh axis runs over, the one named last changes fastest.
Arguments:
- orbitals: float32 [192, 768, 8, 128], P('orb', 'dom')
- potential: float32 [768, 8, 128], P('dom'), may hold values from -3 to 1
- proj_index: int32 [64, 96], replicated, may hold values from 0 to 786431, as said below
- proj_values: float32 [64, 96], replicated, may hold values from -0.625 to 0.625
- proj_energy: float32 [64], replicated, may hold values from 5 to 20
Outputs:
- filtered: float32 [192, 768, 8, 128], P('orb', 'dom')
- hamiltonian_sub: float32 [192, 192], P('orb')
- correlation_sub: float32 [192, 192], P('orb')
Inputs may be any that keep to these rules, and one draw needn't show every extreme that they name: `proj_index`: row a lists, ordered along the first dimension then the second then the third, the 96 cells of a box of 6 x 4 x 4 cells inside the grid; the box's first coordinate is at most 762 and otherwise lies within the slab of cells a // 2 * 24 to a // 2 * 24 + 23.
All inputs are finite; a program needn't handle non-finite values.
Results may differ from a plain program's by a relative error of at most 0.00005.
Values sent between devices are 32-bit elements; how exact they have to be, the bound alone decides.
A program may use at most 128 MiB of HBM per device.

v0:
```python
import jax
import jax.numpy as jnp
from jax import lax
from jax.sharding import PartitionSpec as P

HALO = 6


CENTER_WEIGHT = -5369.0 / 1800.0
SIDE_WEIGHTS = (12.0 / 7.0, -15.0 / 56.0, 10.0 / 189.0, -1.0 / 112.0, 2.0 / 1925.0, -1.0 / 16632.0)
LOWER_BOUND = -1.0
CUT_BOUND = 2.0
UPPER_BOUND = 16.0
HALF_WIDTH = (UPPER_BOUND - CUT_BOUND) / 2.0
MIDDLE = (UPPER_BOUND + CUT_BOUND) / 2.0
SIGMA_ONE = HALF_WIDTH / (LOWER_BOUND - MIDDLE)
SIGMA_TWO = 1.0 / (2.0 / SIGMA_ONE - SIGMA_ONE)


def padded_2(block, sides, width):
    for axis, dim in sides:
        count = lax.axis_size(axis)
        forward = [(i, i + 1) for i in range(count - 1)]
        backward = [(target, source) for source, target in forward]
        low = lax.ppermute(
            lax.slice_in_dim(block, block.shape[dim] - width, None, axis=dim), axis, forward
        )
        high = lax.ppermute(lax.slice_in_dim(block, 0, width, axis=dim), axis, backward)
        block = jnp.concatenate([low, block, high], axis=dim)
    return block


def laplace(center, padded):
    slab_x, span_y, span_z = (center.shape[1], center.shape[2], center.shape[3])
    wide_y = jnp.pad(center, ((0, 0), (0, 0), (HALO, HALO), (0, 0)))
    wide_z = jnp.pad(center, ((0, 0), (0, 0), (0, 0), (HALO, HALO)))
    summed = 3.0 * CENTER_WEIGHT * center
    for shift_by in range(1, HALO + 1):
        weight = SIDE_WEIGHTS[shift_by - 1]
        neighbours = (
            padded[:, HALO + shift_by : HALO + shift_by + slab_x]
            + padded[:, HALO - shift_by : HALO - shift_by + slab_x]
        )
        neighbours = (
            neighbours
            + wide_y[:, :, HALO + shift_by : HALO + shift_by + span_y]
            + wide_y[:, :, HALO - shift_by : HALO - shift_by + span_y]
        )
        neighbours = (
            neighbours
            + wide_z[:, :, :, HALO + shift_by : HALO + shift_by + span_z]
            + wide_z[:, :, :, HALO - shift_by : HALO - shift_by + span_z]
        )
        summed = summed + weight * neighbours
    return summed


def nonlocal_terms(flat_field, proj_index, proj_values, offset):
    cell_count = flat_field.shape[1]
    local_index = proj_index - offset
    inside = (local_index >= 0) & (local_index < cell_count)
    safe_index = jnp.where(inside, local_index, 0)
    weights = jnp.where(inside, proj_values, jnp.zeros_like(proj_values))
    picked = flat_field[:, safe_index]
    return (jnp.sum(picked * weights[None], axis=2), safe_index, weights)


def add_back(flat_field, safe_index, weights, proj_energy, totals):
    spread_back = weights[None] * (proj_energy[None, :, None] * totals[:, :, None])
    return jnp.zeros_like(flat_field).at[:, safe_index].add(spread_back)


def apply_hamiltonian(field, potential, proj_index, proj_values, proj_energy):
    padded = padded_2(field, (("dom", 1),), HALO)
    laplacian = laplace(field, padded)
    flat_field = field.reshape(field.shape[0], -1)
    offset = lax.axis_index("dom") * flat_field.shape[1]
    partial_value, safe_index, weights = nonlocal_terms(flat_field, proj_index, proj_values, offset)
    totals = lax.psum(partial_value, "dom")
    nonlocal_part = add_back(flat_field, safe_index, weights, proj_energy, totals).reshape(
        field.shape
    )
    return -0.5 * laplacian + potential[None] * field + nonlocal_part


def on_device(orbitals, potential, proj_index, proj_values, proj_energy):
    image_one = apply_hamiltonian(orbitals, potential, proj_index, proj_values, proj_energy)
    filtered_one = SIGMA_ONE / HALF_WIDTH * (image_one - MIDDLE * orbitals)
    image_two = apply_hamiltonian(filtered_one, potential, proj_index, proj_values, proj_energy)
    filtered = (
        2.0 * SIGMA_TWO / HALF_WIDTH * (image_two - MIDDLE * filtered_one)
        - SIGMA_ONE * SIGMA_TWO * orbitals
    )
    image_three = apply_hamiltonian(filtered, potential, proj_index, proj_values, proj_energy)
    group_size = filtered.shape[0]
    flat_filtered = filtered.reshape(group_size, -1)
    flat_images = image_three.reshape(group_size, -1)
    total_cells = flat_filtered.shape[1] * lax.axis_size("dom")
    stacked = jnp.stack([flat_filtered, flat_images])
    shard_rows = lax.all_gather(filtered, "orb", axis=0, tiled=True)
    flat_rows = shard_rows.reshape(shard_rows.shape[0], -1)
    partial_gram = jnp.einsum("soc,kc->sok", stacked, flat_rows, precision=lax.Precision.HIGHEST)
    gram_pair = lax.psum(partial_gram, "dom") / total_cells
    return (filtered, gram_pair[1], gram_pair[0])


def solution(mesh):
    in_specs = (P("orb", "dom", None, None), P("dom", None, None), P(), P(), P())
    out_specs = (P("orb", "dom", None, None), P("orb", None), P("orb", None))
    return jax.shard_map(
        on_device, mesh=mesh, in_specs=in_specs, out_specs=out_specs, check_vma=False
    )
```

profile of v0, /device:TPU:1, one launch (start us, length us, event | category | flops | bytes accessed | tf_op | source)
XLA Modules:
  0.0 1110.7 jit_solution(8738105779137120002)
XLA Ops:
  7.2 0.0 all-gather.2.cloned.1.call-start
  7.2 2.5 fusion.168
  9.7 6.2 collective-permute-start.1
  15.9 1.9 collective-permute-start
  17.9 6.8 copy.14
  24.7 0.1 reshape.71
  24.8 25.5 %gather_fusion = f32[6144,24]{1,0:T(8,128)} fusion(f32[24,24576]{0,1:T(8,128)} %bitcast.35, s32[6144]{0:T(1024)S(1)} %broadcast_clamp_fusion), kind=kCustom, calls=%fused_computation | custom fusion | bytes 1204224 | tf_op jit(solution)/shard_map/gather | solution.py:64
  50.3 2.4 multiply_reduce_fusion.2
  52.7 128.3 %psum.28 = f32[24,64]{0,1:T(8,128)S(1)} all-reduce(f32[24,64]{0,1:T(8,128)S(1)} %bitcast.45), channel_id=1, replica_groups=mesh['dom'=32,'orb'=8] {'dom'}, use_global_device_ids=true, to_apply=%region_1.2 | all-reduce | flops 1536 | bytes 12288 | tf_op jit(solution)/shard_map/psum | solution.py:79
  181.0 0.1 broadcast_multiply_fusion.8
  181.0 2.1 broadcast_multiply_fusion.2
  183.2 48.2 %scatter_custom_fusion = f32[24,24576]{0,1:T(8,128)} fusion(s32[6144]{0:T(1024)S(1)} %reshape.71, f32[6144,24]{1,0:T(8,128)} %bitcast.42, f32[]{:T(128)} %constant.21.clone.1), kind=kCustom, calls=%fused_computation.102 | custom fusion | flops 147456 | bytes 2359808 | tf_op jit(solution)/shard_map/scatter-add | solution.py:70
  231.4 8.6 copy.15
  240.0 1.1 constant_dynamic-update-slice_fusion.3
  241.1 0.4 constant_dynamic-update-slice_fusion.1
  241.6 9.8 broadcast_multiply_fusion.3
  251.3 7.6 copy.16
  258.9 2.4 fusion.167
  261.3 25.5 %gather_fusion.1 = f32[6144,24]{1,0:T(8,128)} fusion(f32[24,24576]{0,1:T(8,128)} %bitcast.36, s32[6144]{0:T(1024)S(1)} %broadcast_clamp_fusion), kind=kCustom, calls=%fused_computation.1 | custom fusion | bytes 1204224 | tf_op jit(solution)/shard_map/gather | solution.py:64
  286.7 5.1 collective-permute-start.3
  291.8 4.1 collective-permute-start.2
  296.0 2.4 multiply_reduce_fusion.1
  298.3 124.0 %psum.29 = f32[24,64]{0,1:T(8,128)S(1)} all-reduce(f32[24,64]{0,1:T(8,128)S(1)} %bitcast.46), channel_id=1, replica_groups=mesh['dom'=32,'orb'=8] {'dom'}, use_global_device_ids=true, to_apply=%region_4.5 | all-reduce | flops 1536 | bytes 12288 | tf_op jit(solution)/shard_map/psum | solution.py:79
  422.4 0.1 broadcast_multiply_fusion.7
  422.4 2.1 broadcast_multiply_fusion.1
  424.6 48.2 %scatter_custom_fusion.1 = f32[24,24576]{0,1:T(8,128)} fusion(s32[6144]{0:T(1024)S(1)} %reshape.71, f32[6144,24]{1,0:T(8,128)} %bitcast.43, f32[]{:T(128)} %constant.21.clone.1), kind=kCustom, calls=%fused_computation.100 | custom fusion | flops 147456 | bytes 2359808 | tf_op jit(solution)/shard_map/scatter-add | solution.py:70
  472.8 8.6 copy.17
  481.4 49.0 %fusion.73 = f32[24,24,8,128]{3,2,1,0:T(8,128)} fusion(f32[24,24,8,128]{3,2,1,0:T(8,128)} %copy.17, f32[24,24,8,128]{3,2,1,0:T(8,128)} %get-tuple-element.3, f32[24,6,8,128]{3,2,1,0:T(8,128)S(1)} %collective-permute-done.3, f32[24,6,8,128]{3,2,1,0:T(8,128)} %collective-permute-done.2, f32[24,24,8,128]{3,2,1,0:T(8,128)S(1)} %copy-done.1, ...), kind=kLoop, calls=%fused_computation.194 | loop fusion | flops 37748736 | bytes 13074432 | tf_op jit(solution)/shard_map/sub | solution.py:91
  530.3 0.0 all-gather.2.cloned.1.call-update
  530.4 1.6 copy-done
  532.0 6.8 copy.18
  538.8 25.5 %gather_fusion.2 = f32[6144,24]{1,0:T(8,128)} fusion(f32[24,24576]{0,1:T(8,128)} %bitcast.37, s32[6144]{0:T(1024)S(1)} %broadcast_clamp_fusion), kind=kCustom, calls=%fused_computation.2 | custom fusion | bytes 1204224 | tf_op jit(solution)/shard_map/gather | solution.py:64
  564.3 1.1 fusion.166
  565.4 5.1 collective-permute-start.5
  570.5 4.1 collective-permute-start.4
  574.6 2.4 multiply_reduce_fusion
  577.0 1.8 stack_reshape.6
  578.8 283.8 %psum.30 = f32[24,64]{0,1:T(8,128)S(1)} all-reduce(f32[24,64]{0,1:T(8,128)S(1)} %bitcast.44), channel_id=1, replica_groups=mesh['dom'=32,'orb'=8] {'dom'}, use_global_device_ids=true, to_apply=%region_7.8 | all-reduce | flops 1536 | bytes 12288 | tf_op jit(solution)/shard_map/psum | solution.py:79
  862.6 0.1 broadcast_multiply_fusion.6
  862.7 2.1 broadcast_multiply_fusion
  864.8 48.2 %scatter_custom_fusion.2 = f32[24,24576]{0,1:T(8,128)} fusion(s32[6144]{0:T(1024)S(1)} %reshape.71, f32[6144,24]{1,0:T(8,128)} %bitcast.41, f32[]{:T(128)} %constant.21.clone.1), kind=kCustom, calls=%fused_computation.98 | custom fusion | flops 147456 | bytes 2359808 | tf_op jit(solution)/shard_map/scatter-add | solution.py:70
  913.0 8.6 copy.19
  921.6 9.9 fusion.21
  931.5 3.1 stack_reshape.7
  934.7 17.9 %reshape.105 = f32[192,24576,1]{1,0,2:T(8,128)} reshape(f32[192,24,8,128]{3,2,1,0:T(8,128)} %all-gather.2.cloned.1.call-done) | data formatting | bytes 37748736 | tf_op jit(solution)/shard_map/reshape | solution.py:101
  952.6 22.1 %fusion.6 = f32[2,24,192]{2,1,0:T(8,128)S(1)} fusion(f32[192,24576,1]{1,0,2:T(8,128)} %reshape.105, f32[1,24,24576]{2,1,0:T(8,128)} %stack_reshape.7, f32[1,24,24576]{2,1,0:T(8,128)S(1)} %copy-done.2), kind=kOutput, calls=%fused_computation.104 | convolution fusion | flops 2719088640 | bytes 23629824 | tf_op jit(solution)/shard_map/soc,kc->sok/dot_general | solution.py:102
  974.7 128.5 %psum.31 = f32[2,24,192]{2,1,0:T(8,128)S(1)} all-reduce(f32[2,24,192]{2,1,0:T(8,128)S(1)} %fusion.6), channel_id=1, replica_groups=mesh['dom'=32,'orb'=8] {'dom'}, use_global_device_ids=true, to_apply=%region_9.10 | all-reduce | flops 9216 | bytes 73728 | tf_op jit(solution)/shard_map/psum | solution.py:103
  1103.2 0.6 slice_bitcast_fusion
  (26 shorter events, 0.1 us)
Async XLA Ops:
  7.2 10.7 copy-start.1
  7.2 927.5 %all-gather.2.cloned.1.call-start = ((), (), s32[]{:S(2)}) async-start(), calls=%async_computation | async-start | bytes 21233664 | tf_op jit(solution)/shard_map/all_gather | solution.py:100
  9.7 230.3 %collective-permute-start.1 = (f32[24,6,8,128]{3,2,1,0:T(8,128)}, f32[24,6,8,128]{3,2,1,0:T(8,128)}, u32[]{:S(2)}, u32[]{:S(2)}) collective-permute-start(f32[24,6,8,128]{3,2,1,0:T(8,128)} %get-tuple-element.10), channel_id=1, source_target_pairs={{0,8},{8,16},{16,24},{24,32},{32,40},{40,48},{48,56},{56,64},{64,7... | collective-permute-start | bytes 1769480 | tf_op jit(solution)/shard_map/ppermute | solution.py:25
  15.9 225.6 %collective-permute-start = (f32[24,6,8,128]{3,2,1,0:T(8,128)}, f32[24,6,8,128]{3,2,1,0:T(8,128)S(1)}, u32[]{:S(2)}, u32[]{:S(2)}) collective-permute-start(f32[24,6,8,128]{3,2,1,0:T(8,128)} %get-tuple-element.9), channel_id=1, source_target_pairs={{8,0},{16,8},{24,16},{32,24},{40,32},{48,40},{56,48},{64,56},{72,6... | collective-permute-start | bytes 1769480 | tf_op jit(solution)/shard_map/ppermute | solution.py:28
  17.9 6.8 copy-start.4
  17.9 6.9 copy-start.5
  50.2 130.7 %copy-start.6 = (f32[64]{0:T(128)S(1)}, f32[64]{0:T(128)}, u32[]{:S(2)}) copy-start(f32[64]{0:T(128)} %param.9) | copy-start | bytes 772
  231.4 8.6 copy-start.3
  286.7 194.6 %collective-permute-start.3 = (f32[24,6,8,128]{3,2,1,0:T(8,128)}, f32[24,6,8,128]{3,2,1,0:T(8,128)S(1)}, u32[]{:S(2)}, u32[]{:S(2)}) collective-permute-start(f32[24,6,8,128]{3,2,1,0:T(8,128)} %get-tuple-element.8), channel_id=1, source_target_pairs={{0,8},{8,16},{16,24},{24,32},{32,40},{40,48},{48,56},{56,64},{64,7... | collective-permute-start | bytes 1769480 | tf_op jit(solution)/shard_map/ppermute | solution.py:25
  291.8 189.5 %collective-permute-start.2 = (f32[24,6,8,128]{3,2,1,0:T(8,128)}, f32[24,6,8,128]{3,2,1,0:T(8,128)}, u32[]{:S(2)}, u32[]{:S(2)}) collective-permute-start(f32[24,6,8,128]{3,2,1,0:T(8,128)} %get-tuple-element.7), channel_id=1, source_target_pairs={{8,0},{16,8},{24,16},{32,24},{40,32},{48,40},{56,48},{64,56},{72,6... | collective-permute-start | bytes 1769480 | tf_op jit(solution)/shard_map/ppermute | solution.py:28
  530.3 1.7 copy-start
  565.4 356.2 %collective-permute-start.5 = (f32[24,6,8,128]{3,2,1,0:T(8,128)}, f32[24,6,8,128]{3,2,1,0:T(8,128)S(1)}, u32[]{:S(2)}, u32[]{:S(2)}) collective-permute-start(f32[24,6,8,128]{3,2,1,0:T(8,128)} %get-tuple-element.6), channel_id=1, source_target_pairs={{0,8},{8,16},{16,24},{24,32},{32,40},{40,48},{48,56},{56,64},{64,7... | collective-permute-start | bytes 1769480 | tf_op jit(solution)/shard_map/ppermute | solution.py:25
  570.5 351.1 %collective-permute-start.4 = (f32[24,6,8,128]{3,2,1,0:T(8,128)}, f32[24,6,8,128]{3,2,1,0:T(8,128)}, u32[]{:S(2)}, u32[]{:S(2)}) collective-permute-start(f32[24,6,8,128]{3,2,1,0:T(8,128)} %get-tuple-element.5), channel_id=1, source_target_pairs={{8,0},{16,8},{24,16},{32,24},{40,32},{48,40},{56,48},{64,56},{72,6... | collective-permute-start | bytes 1769480 | tf_op jit(solution)/shard_map/ppermute | solution.py:28
  934.7 17.9 %copy-start.2 = (f32[1,24,24576]{2,1,0:T(8,128)S(1)}, f32[1,24,24576]{2,1,0:T(8,128)}, u32[]{:S(2)}) copy-start(f32[1,24,24576]{2,1,0:T(8,128)} %stack_reshape.6) | copy-start | bytes 7077892
Sparse Core Ops, SparseCore 0:
  530.5 209.8 all-gather.1
where the time goes:
time: 1120 us; the launch traced here: 1110 us
  blocking collectives  665 us (59%)
  other arithmetic  227 us (20%)
  local copies, waits for them, and re-layouts  156 us (14%)
  starting transfers between devices  26.6 us (2%)
  matrix products  22.1 us (2%)
  between operations  14.2 us (1%)
    psum x3, blocking collectives, apply_hamiltonian(): totals = lax.psum(partial_value, 'dom')  536 us
    scatter-add x3, other arithmetic, add_back(): return jnp.zeros_like(flat_field).at[:, safe_index].add(spread_back)  145 us
    psum x1, blocking collectives, on_device(): gram_pair = lax.psum(partial_gram, 'dom') / total_cells  129 us
    gather x3, local copies, waits for them, and re-layouts, nonlocal_terms(): picked = flat_field[:, safe_index]  76.4 us
    sub x1, other arithmetic, on_device(): 2.0 * SIGMA_TWO / HALF_WIDTH * (image_two - MIDDLE * filtered_one)  49 us
    reshape x3, local copies, waits for them, and re-layouts, apply_hamiltonian(): add_back(flat_field, safe_index, weights, proj_energy, totals)  25.7 us
  transfers between devices with their start and end apart: 7, of which 0 were waited for; matrix products, arithmetic and copies ran while one was open for 24% of the time, Pallas kernels for 0%

commit v1 on v0

v1 whole, which is shorter than its diff:
```python
import functools

import jax
import jax.numpy as jnp
import numpy as np
from jax import lax
from jax.experimental import pallas as pl
from jax.experimental.pallas import tpu as pltpu
from jax.sharding import PartitionSpec as P

MESH = pl.DeviceIdType.MESH
F32 = jnp.float32
BF16 = jnp.bfloat16

CENTER_WEIGHT = -5369.0 / 1800.0
SIDE_WEIGHTS = (12.0 / 7.0, -15.0 / 56.0, 10.0 / 189.0, -1.0 / 112.0, 2.0 / 1925.0, -1.0 / 16632.0)
LOWER_BOUND = -1.0
CUT_BOUND = 2.0
UPPER_BOUND = 16.0
HALF_WIDTH = (UPPER_BOUND - CUT_BOUND) / 2.0
MIDDLE = (UPPER_BOUND + CUT_BOUND) / 2.0
SIGMA_ONE = HALF_WIDTH / (LOWER_BOUND - MIDDLE)
SIGMA_TWO = 1.0 / (2.0 / SIGMA_ONE - SIGMA_ONE)

ORB = 24
CX = 24
HALO = 6
NY = 8
NZ = 128
ROWS = CX * NY
EDGE = HALO * NY
PAD = ROWS + 2 * EDGE
NQ = 4
OQ = ORB // NQ
NX4 = 4
XL = CX // NX4
XR = XL * NY
XA, XB = 32, 16
W = NX4 * ORB
K = XR * NZ
NDOM = 32
SIDE = tuple(-0.5 * w for w in SIDE_WEIGHTS)
DIAG = -0.5 * 3.0 * CENTER_WEIGHT


def band(n):
    m = np.zeros((n, n), np.float64)
    for k, w in enumerate(SIDE, 1):
        m += w * (np.eye(n, k=k) + np.eye(n, k=-k))
    return m


def constants():
    bz = jnp.asarray(band(NZ), F32)
    hi = bz.astype(BF16)
    lo = (bz - hi.astype(F32)).astype(BF16)
    wz = jnp.concatenate(
        [jnp.concatenate([hi, lo], 1), jnp.concatenate([hi, jnp.zeros_like(lo)], 1)], 0
    )
    by = band(NY)
    cy = np.zeros((NY, NY, NZ), np.float32)
    for s in range(NY):
        for y in range(NY):
            cy[s, y, :] = by[y, (y - s) % NY]
    return wz, jnp.asarray(cy)


def kernel(
    x_ref, pot_ref, idx_ref, val_ref, en_ref, wz_ref, cy_ref,
    out_ref, gram_ref,
    p0, p1, p2, im, cf, box, dfo, dfp, tb, pe,
    fa, ia, fo, fb, ib, ob, snd_own, snd_x, rcv_own, rcv_x, red, a2, a3, mine,
    loc_sem, hs, hr, fs, fr, gs, gr, ys, yr, vs, vr, r1s, r1r, r2s, r2r, r3s, r3r, r4s, r4r,
):
    dom = lax.axis_index("dom")
    orb = lax.axis_index("orb")
    row = orb // NX4
    xx = orb % NX4
    zz = dom // 4
    tt = dom % 4
    up = lax.rem(dom + 1, NDOM)
    down = lax.rem(dom + NDOM - 1, NDOM)
    other = (1 - row) * NX4

    def xpeer(k):
        return lax.rem(xx + k, NX4)

    barrier = pltpu.get_barrier_semaphore()
    peers = [(up, orb), (down, orb)]
    peers += [(dom, row * NX4 + xpeer(k)) for k in range(1, 4)]
    peers += [(dom, other + xpeer(k)) for k in range(4)]
    peers += [(zz * 4 + lax.rem(tt + k, 4), orb) for k in range(1, 4)]
    peers += [(lax.rem(zz + k, 8) * 4 + tt, orb) for k in range(1, 8)]
    for peer in peers:
        pl.semaphore_signal(barrier, inc=1, device_id=peer, device_id_type=MESH)

    load = pltpu.make_async_copy(x_ref, p0.at[:, pl.ds(EDGE, ROWS), :], loc_sem.at[0])
    load.start()
    pl.semaphore_wait(barrier, len(peers))

    def remote(src, dst, send, recv, device):
        return pltpu.make_async_remote_copy(
            src_ref=src, dst_ref=dst, send_sem=send, recv_sem=recv, device_id=device, device_id_type=MESH
        )

    def halo(field, src, base, q, way):
        part = pl.ds(q * OQ, OQ)
        if way == 0:
            s = src.at[part, pl.ds(base + ROWS - EDGE, EDGE), :]
            d = (p0, p1, p2)[field].at[part, pl.ds(0, EDGE), :]
            to = (up, orb)
        else:
            s = src.at[part, pl.ds(base, EDGE), :]
            d = (p0, p1, p2)[field].at[part, pl.ds(EDGE + ROWS, EDGE), :]
            to = (down, orb)
        return remote(s, d, hs.at[field, way, q], hr.at[field, way, q], to)

    def halo_start(field, src, base, q):
        @pl.when(dom < NDOM - 1)
        def _():
            halo(field, src, base, q, 0).start()

        @pl.when(dom > 0)
        def _():
            halo(field, src, base, q, 1).start()

    def halo_recv(field, src, base, q):
        @pl.when(dom > 0)
        def _():
            halo(field, src, base, q, 0).wait_recv()

        @pl.when(dom < NDOM - 1)
        def _():
            halo(field, src, base, q, 1).wait_recv()

    def halo_sent(field, src, base, q):
        @pl.when(dom < NDOM - 1)
        def _():
            halo(field, src, base, q, 0).wait_send()

        @pl.when(dom > 0)
        def _():
            halo(field, src, base, q, 1).wait_send()

    def loop(n, body):
        lax.fori_loop(0, n, lambda i, c: (body(i), c)[1], 0)

    loop(NQ, lambda q: halo_start(0, x_ref, 0, q))

    @pl.when(dom == 0)
    def _():
        for p in (p0, p1, p2):
            p[:, 0:EDGE, :] = jnp.zeros((ORB, EDGE, NZ), F32)

    @pl.when(dom == NDOM - 1)
    def _():
        for p in (p0, p1, p2):
            p[:, EDGE + ROWS :, :] = jnp.zeros((ORB, EDGE, NZ), F32)

    cf[...] = pot_ref[...] + (DIAG - MIDDLE)
    for buf in (fb, ib, ob):
        for h in (0, 128):
            buf[h + W : h + 128, :] = jnp.zeros((128 - W, buf.shape[1]), BF16)

    sub = lax.broadcasted_iota(jnp.int32, (NY, NZ), 0)
    lane = lax.broadcasted_iota(jnp.int32, (NY, NZ), 1)

    def atom_id(a):
        return jnp.where(a < 2, 2 * dom + a, jnp.maximum(2 * dom - 4 + a, 0))

    def start_of(a):
        first = idx_ref[atom_id(a), 0]
        return first // (NY * NZ) - CX * dom, first // NZ % NY, first % NZ

    def build_box(a):
        _, y0, z0 = start_of(a)
        dy = sub - y0
        dz = lane - z0

        def layer(l):
            d = jnp.zeros((NY, NZ), F32)
            for j in range(4):
                for k in range(4):
                    d = jnp.where((dy == j) & (dz == k), val_ref[atom_id(a), l * 16 + j * 4 + k], d)
            box[a, l] = d

        loop(6, layer)

    loop(4, build_box)

    def place(a, x):
        x0, _, _ = start_of(a)
        off = jnp.zeros((NY, NZ), jnp.int32) + (x - x0)
        d = jnp.zeros((NY, NZ), F32)
        for l in range(6):
            d = jnp.where(off == l, box[a, l], d)
        return d

    def place_own(x):
        for a in range(2):
            dfo[a, x] = place(a, x)

    def place_low(i):
        for a in range(2):
            dfp[a, i] = place(a + 2, i - 5)

    loop(29, place_own)
    loop(10, place_low)

    def inner(p, n):
        def body(o):
            c = p[o, EDGE : EDGE + ROWS, :]
            hi = c.astype(BF16)
            lo = (c - hi.astype(F32)).astype(BF16)
            z = jnp.dot(jnp.concatenate([hi, lo], 1), wz_ref[...], preferred_element_type=F32)
            z = z[:, :NZ] + z[:, NZ:]
            t = [jnp.zeros((NY, NZ), F32)] * 4
            for x0 in range(0, CX, 8):
                first, last = max(x0 - HALO, 0), min(x0 + 8 + HALO, CX)
                blk = p[o, EDGE + first * NY : EDGE + last * NY, :].reshape(last - first, NY, NZ)
                zero = jnp.zeros((8 + 2 * HALO - (last - first), NY, NZ), F32)
                if x0 - HALO < 0:
                    blk = jnp.concatenate([zero, blk], 0)
                elif x0 + 8 + HALO > CX:
                    blk = jnp.concatenate([blk, zero], 0)
                ctr = blk[HALO : HALO + 8]
                rows = slice(x0 * NY, (x0 + 8) * NY)
                s = cf[rows, :].reshape(8, NY, NZ) * ctr + z[rows, :].reshape(8, NY, NZ)
                for k in range(1, HALO + 1):
                    s = s + SIDE[k - 1] * (blk[HALO + k : HALO + 8 + k] + blk[HALO - k : HALO + 8 - k])
                for r in range(1, NY):
                    s = s + cy_ref[r][None] * pltpu.roll(ctr, r, 1)
                n[o, pl.ds(EDGE + x0 * NY, 8 * NY), :] = s.reshape(8 * NY, NZ)
                for a in range(2):
                    t[a] = t[a] + jnp.sum(dfo[a, x0 : x0 + 8] * ctr, axis=0)
                    if x0 == 0:
                        t[2 + a] = jnp.sum(dfp[a, 5:10] * ctr[0:5], axis=0)
            for a in range(4):
                tb[o, a] = t[a]

        loop(ORB, body)

    def outer(p, n, q, scale, extra):
        def body(i):
            o = q * OQ + i
            low = p[o, 0:EDGE, :].reshape(HALO, NY, NZ)
            high = p[o, EDGE + ROWS : PAD, :].reshape(HALO, NY, NZ)
            for a in range(2):
                tb[o, a] = tb[o, a] + jnp.sum(dfo[a, 24:29] * high[0:5], axis=0)
                tb[o, 2 + a] = tb[o, 2 + a] + jnp.sum(dfp[a, 0:5] * low[1:6], axis=0)
            first = [jnp.zeros((NY, NZ), F32)] * HALO
            last = [jnp.zeros((NY, NZ), F32)] * HALO
            for k in range(1, HALO + 1):
                for x in range(k):
                    first[x] = first[x] + SIDE[k - 1] * low[HALO - k + x]
                    last[HALO - k + x] = last[HALO - k + x] + SIDE[k - 1] * high[x]
            add = jnp.concatenate(first, 0)
            n[o, pl.ds(EDGE, EDGE), :] = n[o, pl.ds(EDGE, EDGE), :] + add
            add = jnp.concatenate(last, 0)
            n[o, pl.ds(ROWS, EDGE), :] = n[o, pl.ds(ROWS, EDGE), :] + add

        loop(OQ, body)
        part = pl.ds(q * OQ, OQ)
        total = jnp.sum(jnp.sum(tb[part], axis=3, keepdims=True), axis=2, keepdims=True)
        for a in range(4):
            e = en_ref[0, atom_id(a)]
            if a >= 2:
                e = jnp.where(dom > 0, e, 0.0)
            pe[part, a] = jnp.broadcast_to(total[:, a] * e, (OQ, NY, NZ))

        def finish(i):
            o = q * OQ + i
            for x0 in range(0, CX, 8):
                rows = pl.ds(EDGE + x0 * NY, 8 * NY)
                s = n[o, rows, :].reshape(8, NY, NZ)
                for a in range(2):
                    s = s + dfo[a, x0 : x0 + 8] * pe[o, a][None]
                if x0 == 0:
                    t = s[0:5]
                    for a in range(2):
                        t = t + dfp[a, 5:10] * pe[o, 2 + a][None]
                    s = jnp.concatenate([t, s[5:8]], 0)
                if extra == 2:
                    s = scale * s - (SIGMA_ONE * SIGMA_TWO) * p0[o, rows, :].reshape(8, NY, NZ)
                elif extra == 1:
                    s = scale * s
                else:
                    s = s + MIDDLE * p[o, rows, :].reshape(8, NY, NZ)
                n[o, rows, :] = s.reshape(8 * NY, NZ)

        loop(OQ, finish)

    load.wait()
    inner(p0, p1)

    def step_one(q):
        halo_recv(0, x_ref, 0, q)
        outer(p0, p1, q, SIGMA_ONE / HALF_WIDTH, 1)
        halo_start(1, p1, EDGE, q)

    loop(NQ, step_one)

    def gather(src, dst, send, recv, q, k):
        s = src.at[pl.ds(q * OQ, OQ), pl.ds(pl.multiple_of(EDGE + xpeer(k) * XR, 8), XR), :]
        d = dst.at[pl.ds(xx * ORB + q * OQ, OQ), :, :]
        return remote(s, d, send.at[q, k], recv.at[q, k], (dom, row * NX4 + xpeer(k)))

    def keep(src, dst, sem, q):
        s = src.at[pl.ds(q * OQ, OQ), pl.ds(pl.multiple_of(EDGE + xx * XR, 8), XR), :]
        return pltpu.make_async_copy(s, dst.at[pl.ds(xx * ORB + q * OQ, OQ), :, :], sem)

    def store(q):
        part = pl.ds(q * OQ, OQ)
        return pltpu.make_async_copy(
            p2.at[part, pl.ds(EDGE, ROWS), :], out_ref.at[part, :, :], loc_sem.at[1 + q]
        )

    def cross(src, to, rows, q, k, send, recv):
        who = lax.rem(xx + NX4 - k, NX4)
        part = pl.ds(who * ORB + q * OQ, OQ)
        return remote(
            src.at[part, rows, :], fo.at[part, to, :], send.at[q, k], recv.at[q, k], (dom, other + xx)
        )

    def cross_low(q, k):
        return cross(fa, pl.ds(0, XA), pl.ds(0, XA), q, k, ys, yr)

    def cross_high(q, k):
        return cross(fa, pl.ds(0, XB), pl.ds(XA, XB), q, k, ys, yr)

    def cross_image(q, k):
        return cross(ia, pl.ds(XB, XB), pl.ds(XA, XB), q, k, vs, vr)

    def by_row(zero, one):
        if zero is not None:
            pl.when(row == 0)(zero)
        if one is not None:
            pl.when(row == 1)(one)

    inner(p1, p2)

    def step_two(q):
        halo_recv(1, p1, EDGE, q)
        outer(p1, p2, q, 2.0 * SIGMA_TWO / HALF_WIDTH, 2)
        halo_start(2, p2, EDGE, q)
        for k in range(1, 4):
            gather(p2, fa, fs, fr, q, k).start()
        keep(p2, fa, fs.at[q, 0], q).start()
        store(q).start()

    loop(NQ, step_two)

    inner(p2, im)

    def step_three(q):
        halo_recv(2, p2, EDGE, q)
        outer(p2, im, q, 1.0, 0)
        for k in range(1, 4):
            gather(im, ia, gs, gr, q, k).start()
        keep(im, ia, gs.at[q, 0], q).start()

    loop(NQ, step_three)

    def pass_on(q):
        keep(p2, fa, fs.at[q, 0], q).wait()
        for k in range(4):
            if k:
                gather(p2, fa, fs, fr, q, k).wait_recv()
            by_row(lambda: cross_high(q, k).start(), lambda: cross_low(q, k).start())

    loop(NQ, pass_on)

    def arrived(q):
        for k in range(4):
            by_row(lambda: cross_low(q, k).wait_recv(), lambda: cross_high(q, k).wait_recv())

    def split(src, height, dst, start, rows):
        flat = src.reshape(W * height, NZ)

        def body(c):
            v = [flat[pl.ds(start + 2 * c + i, W, stride=height), :] for i in range(2)]
            v = jnp.concatenate(v, 1)
            hi = v.astype(BF16)
            at = pl.ds(pl.multiple_of(c * 2 * NZ, 2 * NZ), 2 * NZ)
            dst[0:W, at] = hi
            dst[128 : 128 + W, at] = (v - hi.astype(F32)).astype(BF16)

        loop(rows // 2, body)

    def mul(a, b):
        g = lax.dot_general(a, b, (((1,), (1,)), ((), ())), preferred_element_type=F32)
        g = g[:128] + g[128:]
        return g[:, :128] + g[:, 128:]

    def put(m, h, g):
        snd_own[:, 2 * m + h] = g[:W].reshape(NX4, ORB, 128)
        if h:
            snd_x[:, m] = jnp.transpose(g)[:W].reshape(NX4, ORB, 128)

    split(fa, XR, fb, 0, XR)
    put(1, 0, mul(fb[...], fb[...]))
    loop(NQ, arrived)

    def across_zero():
        split(fo, XA, ob, 0, XA)
        put(1, 1, mul(fb[:, : XA * NZ], ob[...]))

    def across_one():
        split(fo, XA, ob, 0, XB)
        put(1, 1, mul(fb[:, XA * NZ :], ob[:, : XB * NZ]))

    by_row(across_zero, across_one)

    def image_in(q):
        keep(im, ia, gs.at[q, 0], q).wait()
        for k in range(4):
            if k:
                gather(im, ia, gs, gr, q, k).wait_recv()
            by_row(lambda: cross_image(q, k).start(), None)

    loop(NQ, image_in)
    split(ia, XR, ib, 0, XR)
    put(0, 0, mul(ib[...], fb[...]))

    def image_zero():
        put(0, 1, mul(ib[:, : XA * NZ], ob[...]))

    def image_one():
        def wait(q):
            for k in range(4):
                cross_image(q, k).wait_recv()

        loop(NQ, wait)
        split(fo, XA, ob, XB, XB)
        put(0, 1, mul(fb[:, XA * NZ :], ob[:, : XB * NZ]))

    by_row(image_zero, image_one)

    def rows_own(k):
        return remote(
            snd_own.at[xpeer(k)], rcv_own.at[k], r1s.at[k], r1r.at[k], (dom, row * NX4 + xpeer(k))
        )

    def rows_x(k):
        return remote(
            snd_x.at[xpeer(k)], rcv_x.at[k], r1s.at[4 + k], r1r.at[4 + k], (dom, other + xpeer(k))
        )

    for k in range(4):
        rows_x(k).start()
    for k in range(1, 4):
        rows_own(k).start()
    total = snd_own[xx]
    for k in range(1, 4):
        rows_own(k).wait_recv()
        total = total + rcv_own[k]
    cr = jnp.zeros((2, ORB, 128), F32)
    for k in range(4):
        rows_x(k).wait_recv()
        cr = cr + rcv_x[k]
    red[...] = total
    red[1] = total[1] + cr[0]
    red[3] = total[3] + cr[1]

    def quarter(k):
        t = lax.rem(tt + k, 4)
        return remote(red.at[t], a2.at[k], r2s.at[k], r2r.at[k], (zz * 4 + t, orb))

    for k in range(1, 4):
        quarter(k).start()
    s = red[tt]
    for k in range(1, 4):
        quarter(k).wait_recv()
        s = s + a2[k]
    mine[...] = s

    def along(k):
        z = lax.rem(zz + k, 8)
        return remote(mine, a3.at[k], r3s.at[k], r3r.at[k], (z * 4 + tt, orb))

    for k in range(1, 8):
        along(k).start()
    for k in range(1, 8):
        along(k).wait_recv()
        s = s + a3[k]
    gram_ref[tt] = s

    def back(k):
        t = lax.rem(tt + k, 4)
        return remote(gram_ref.at[tt], gram_ref.at[tt], r4s.at[k], r4r.at[k], (zz * 4 + t, orb))

    for k in range(1, 4):
        back(k).start()

    def sent(q):
        halo_sent(0, x_ref, 0, q)
        halo_sent(1, p1, EDGE, q)
        halo_sent(2, p2, EDGE, q)
        store(q).wait()
        for k in range(1, 4):
            gather(p2, fa, fs, fr, q, k).wait_send()
            gather(im, ia, gs, gr, q, k).wait_send()
        for k in range(4):
            by_row(lambda: cross_high(q, k).wait_send(), lambda: cross_low(q, k).wait_send())
            by_row(lambda: cross_image(q, k).wait_send(), None)

    loop(NQ, sent)
    for k in range(1, 4):
        rows_own(k).wait_send()
        quarter(k).wait_send()
        back(k).wait_send()
    for k in range(4):
        rows_x(k).wait_send()
    for k in range(1, 8):
        along(k).wait_send()
    for k in range(1, 4):
        t = lax.rem(tt + 4 - k, 4)
        remote(
            gram_ref.at[t], gram_ref.at[t], r4s.at[k], r4r.at[k], (zz * 4 + t, orb)
        ).wait_recv()


def on_device(orbitals, potential, proj_index, proj_values, proj_energy):
    wz, cy = constants()
    dma = pltpu.SemaphoreType.DMA
    vmem = pl.BlockSpec(memory_space=pltpu.VMEM)
    smem = pl.BlockSpec(memory_space=pltpu.SMEM)
    hbm = pl.BlockSpec(memory_space=pl.ANY)
    filtered, gram = pl.pallas_call(
        kernel,
        out_shape=(
            jax.ShapeDtypeStruct((ORB, ROWS, NZ), F32),
            jax.ShapeDtypeStruct((4, ORB, 128), F32),
        ),
        in_specs=[hbm, vmem, smem, smem, smem, vmem, vmem],
        out_specs=(hbm, vmem),
        scratch_shapes=[
            pltpu.VMEM((ORB, PAD, NZ), F32),
            pltpu.VMEM((ORB, PAD, NZ), F32),
            pltpu.VMEM((ORB, PAD, NZ), F32),
            pltpu.VMEM((ORB, PAD, NZ), F32),
            pltpu.VMEM((ROWS, NZ), F32),
            pltpu.VMEM((4, 6, NY, NZ), F32),
            pltpu.VMEM((2, 29, NY, NZ), F32),
            pltpu.VMEM((2, 10, NY, NZ), F32),
            pltpu.VMEM((ORB, 4, NY, NZ), F32),
            pltpu.VMEM((ORB, 4, NY, NZ), F32),
            pltpu.VMEM((W, XR, NZ), F32),
            pltpu.VMEM((W, XR, NZ), F32),
            pltpu.VMEM((W, XA, NZ), F32),
            pltpu.VMEM((256, K), BF16),
            pltpu.VMEM((256, K), BF16),
            pltpu.VMEM((256, XA * NZ), BF16),
            pltpu.VMEM((NX4, 4, ORB, 128), F32),
            pltpu.VMEM((NX4, 2, ORB, 128), F32),
            pltpu.VMEM((NX4, 4, ORB, 128), F32),
            pltpu.VMEM((NX4, 2, ORB, 128), F32),
            pltpu.VMEM((4, ORB, 128), F32),
            pltpu.VMEM((4, ORB, 128), F32),
            pltpu.VMEM((8, ORB, 128), F32),
            pltpu.VMEM((ORB, 128), F32),
            dma((1 + NQ,)),
            dma((3, 2, NQ)), dma((3, 2, NQ)),
            dma((NQ, 4)), dma((NQ, 4)),
            dma((NQ, 4)), dma((NQ, 4)),
            dma((NQ, 4)), dma((NQ, 4)),
            dma((NQ, 4)), dma((NQ, 4)),
            dma((8,)), dma((8,)),
            dma((4,)), dma((4,)),
            dma((8,)), dma((8,)),
            dma((4,)), dma((4,)),
        ],
        compiler_params=pltpu.CompilerParams(
            collective_id=0, has_side_effects=True, vmem_limit_bytes=56 << 20
        ),
        name="filter_step",
    )(
        orbitals.reshape(ORB, ROWS, NZ),
        potential.reshape(ROWS, NZ),
        proj_index,
        proj_values,
        proj_energy.reshape(1, -1),
        wz,
        cy,
    )
    first = lax.axis_index("orb") < NX4
    cells = ROWS * NZ * lax.axis_size("dom")

    def whole(own, across):
        own, across = own[:, :W], across[:, :W]
        low = jnp.where(first, own, across)
        high = jnp.where(first, across, own)
        return jnp.concatenate([low, high], 1) / cells

    return filtered.reshape(orbitals.shape), whole(gram[0], gram[1]), whole(gram[2], gram[3])


def solution(mesh):
    in_specs = (P("orb", "dom", None, None), P("dom", None, None), P(), P(), P())
    out_specs = (P("orb", "dom", None, None), P("orb", None), P("orb", None))
    return jax.shard_map(
        on_device, mesh=mesh, in_specs=in_specs, out_specs=out_specs, check_vma=False
    )
```

time: 1120 us -> 132 us (0.12)
  blocking collectives: 665 us -> 0 us
  other arithmetic: 227 us -> 1.38 us
  local copies, waits for them, and re-layouts: 156 us -> 4.06 us
  Pallas kernels: 0 us -> 125 us
  starting transfers between devices: 26.6 us -> 0 us
  matrix products: 22.1 us -> 0 us
  between operations: 14.2 us -> 0.64 us
    psum x4 -> x0, blocking collectives: 665 us -> none  [the longest x3 536 us: apply_hamiltonian(): totals = lax.psum(partial_value, 'dom')]
    scatter-add x3 -> x0, other arithmetic: 145 us -> none  [add_back(): return jnp.zeros_like(flat_field).at[:, safe_index].add(spread_back)]
    pallas_call x0 -> x1, Pallas kernels: none -> 125 us  [on_device(): pl.pallas_call(kernel, out_shape=(jax.ShapeDtypeStruct((ORB, ROWS, NZ), F...]
    gather x3 -> x0, local copies, waits for them, and re-layouts: 76.4 us -> none  [nonlocal_terms(): picked = flat_field[:, safe_index]]
    sub x1 -> x0, other arithmetic: 49 us -> none  [on_device(): 2.0 * SIGMA_TWO / HALF_WIDTH * (image_two - MIDDLE * filtered_one)]
    reshape x4 -> x0, local copies, waits for them, and re-layouts: 43.6 us -> none  [the longest x3 25.7 us: apply_hamiltonian(): add_back(flat_field, safe_index, weights, proj_energy, totals)]
    ppermute x6 -> x0, starting transfers between devices: 26.5 us -> none  [the longest x3 16.3 us: padded_2(): lax.ppermute(lax.slice_in_dim(block, block.shape[dim] - width, None, axis...]
    dot_general x1 -> x0, matrix products: 22.1 us -> none  [on_device(): jnp.einsum('soc,kc->sok', stacked, flat_rows, precision=lax.Precision.HIG...]
  transfers between devices with their start and end apart: 7 -> 0, of which waited for: 0 -> 0; matrix products, arithmetic and copies ran while one was open for 24% -> 0% of each run, Pallas kernels for 0% -> 0%
where the time goes in v1:
time: 132 us; the launch traced here: 131 us
  Pallas kernels  125 us (95%)
  local copies, waits for them, and re-layouts  4.06 us (3%)
  other arithmetic  1.38 us (1%)
    pallas_call x1, Pallas kernels, on_device(): pl.pallas_call(kernel, out_shape=(jax.ShapeDtypeStruct((ORB, ROWS, NZ), F...  125 us
    unnamed x1, local copies, waits for them, and re-layouts  3.3 us

profile of v1, /device:TPU:1, one launch (start us, length us, event | category | flops | bytes accessed | tf_op | source)
XLA Modules:
  0.0 130.9 jit_solution(3547389664362218062)
XLA Ops:
  0.6 124.9 %filter_step.1 = (f32[24,192,128]{2,1,0:T(8,128)}, f32[4,24,128]{2,1,0:T(8,128)}) custom-call(f32[24,192,128]{2,1,0:T(8,128)} %bitcast.12, f32[192,128]{1,0:T(8,128)} %bitcast.14, s32[64,96]{1,0:T(8,128)} %idx_ref.1, f32[64,96]{1,0:T(8,128)} %val_ref.1, f32[1,64]{1,0:T(1,128)} %bitcast.15, bf16[256,256]{1,0:T(8,128)(2,1)} %constant.28.wz_ref, ...), custom_call_target="tpu_custom_call" | custom-call | tf_op jit(solution)/shard_map/filter_step/pallas_call | solution.py:529
  125.5 0.8 slice_bitcast_fusion.1
  126.3 0.7 maximum_multiply_fusion.1
  127.0 0.7 maximum_multiply_fusion
  127.6 3.3 %copy.11 = f32[24,24,8,128]{3,2,1,0:T(8,128)} copy(f32[24,24,8,128]{3,2,1,0:T(8,128)} %bitcast.13) | data formatting | bytes 4718592
  (1 shorter events, 0.0 us)

commit v2 on v1

--- a/solution.py
+++ b/solution.py
@@ -145,7 +145,7 @@
     def loop(n, body):
         lax.fori_loop(0, n, lambda i, c: (body(i), c)[1], 0)
 
-    loop(NQ, lambda q: halo_start(0, x_ref, 0, q))
+    loop(2, lambda q: halo_start(0, x_ref, 0, q))
 
     @pl.when(dom == 0)
     def _():
@@ -207,8 +207,9 @@
     loop(29, place_own)
     loop(10, place_low)
 
-    def inner(p, n):
-        def body(o):
+    def inner(p, n, q):
+        def body(i):
+            o = q * OQ + i
             c = p[o, EDGE : EDGE + ROWS, :]
             hi = c.astype(BF16)
             lo = (c - hi.astype(F32)).astype(BF16)
@@ -238,7 +239,7 @@
             for a in range(4):
                 tb[o, a] = t[a]
 
-        loop(ORB, body)
+        loop(OQ, body)
 
     def outer(p, n, q, scale, extra):
         def body(i):
@@ -290,16 +291,6 @@
 
         loop(OQ, finish)
 
-    load.wait()
-    inner(p0, p1)
-
-    def step_one(q):
-        halo_recv(0, x_ref, 0, q)
-        outer(p0, p1, q, SIGMA_ONE / HALF_WIDTH, 1)
-        halo_start(1, p1, EDGE, q)
-
-    loop(NQ, step_one)
-
     def gather(src, dst, send, recv, q, k):
         s = src.at[pl.ds(q * OQ, OQ), pl.ds(pl.multiple_of(EDGE + xpeer(k) * XR, 8), XR), :]
         d = dst.at[pl.ds(xx * ORB + q * OQ, OQ), :, :]
@@ -337,7 +328,20 @@
         if one is not None:
             pl.when(row == 1)(one)
 
-    inner(p1, p2)
+    def step_one(q):
+        halo_recv(0, x_ref, 0, q)
+        outer(p0, p1, q, SIGMA_ONE / HALF_WIDTH, 1)
+        halo_start(1, p1, EDGE, q)
+
+        @pl.when(q + 2 < NQ)
+        def _():
+            halo_start(0, x_ref, 0, q + 2)
+
+        inner(p1, p2, q)
+
+        @pl.when(q + 1 < NQ)
+        def _():
+            inner(p0, p1, q + 1)
 
     def step_two(q):
         halo_recv(1, p1, EDGE, q)
@@ -347,10 +351,7 @@
             gather(p2, fa, fs, fr, q, k).start()
         keep(p2, fa, fs.at[q, 0], q).start()
         store(q).start()
-
-    loop(NQ, step_two)
-
-    inner(p2, im)
+        inner(p2, im, q)
 
     def step_three(q):
         halo_recv(2, p2, EDGE, q)
@@ -359,8 +360,6 @@
             gather(im, ia, gs, gr, q, k).start()
         keep(im, ia, gs.at[q, 0], q).start()
 
-    loop(NQ, step_three)
-
     def pass_on(q):
         keep(p2, fa, fs.at[q, 0], q).wait()
         for k in range(4):
@@ -368,7 +367,21 @@
                 gather(p2, fa, fs, fr, q, k).wait_recv()
             by_row(lambda: cross_high(q, k).start(), lambda: cross_low(q, k).start())
 
-    loop(NQ, pass_on)
+    def image_in(q):
+        keep(im, ia, gs.at[q, 0], q).wait()
+        for k in range(4):
+            if k:
+                gather(im, ia, gs, gr, q, k).wait_recv()
+            by_row(lambda: cross_image(q, k).start(), None)
+
+    load.wait()
+    inner(p0, p1, 0)
+
+    def wave(i):
+        for lag, step in enumerate((step_one, step_two, step_three, pass_on, image_in)):
+            pl.when((i >= lag) & (i < NQ + lag))(functools.partial(step, i - lag))
+
+    loop(NQ + 4, wave)
 
     def arrived(q):
         for k in range(4):
@@ -399,6 +412,8 @@
 
     split(fa, XR, fb, 0, XR)
     put(1, 0, mul(fb[...], fb[...]))
+    split(ia, XR, ib, 0, XR)
+    put(0, 0, mul(ib[...], fb[...]))
     loop(NQ, arrived)
 
     def across_zero():
@@ -410,17 +425,6 @@
         put(1, 1, mul(fb[:, XA * NZ :], ob[:, : XB * NZ]))
 
     by_row(across_zero, across_one)
-
-    def image_in(q):
-        keep(im, ia, gs.at[q, 0], q).wait()
-        for k in range(4):
-            if k:
-                gather(im, ia, gs, gr, q, k).wait_recv()
-            by_row(lambda: cross_image(q, k).start(), None)
-
-    loop(NQ, image_in)
-    split(ia, XR, ib, 0, XR)
-    put(0, 0, mul(ib[...], fb[...]))
 
     def image_zero():
         put(0, 1, mul(ib[:, : XA * NZ], ob[...]))
@@ -518,6 +522,41 @@
         remote(
             gram_ref.at[t], gram_ref.at[t], r4s.at[k], r4r.at[k], (zz * 4 + t, orb)
         ).wait_recv()
+
+
+def finish(full_ref, gram_ref, out_ref, h_ref, s_ref, hold, gram, pair, sem, small):
+    def copies(i):
+        part = pl.ds(3 * i, 3)
+        return (
+            pltpu.make_async_copy(full_ref.at[part], hold.at[part], sem.at[0, i]),
+            pltpu.make_async_copy(hold.at[part], out_ref.at[part], sem.at[1, i]),
+        )
+
+    load = pltpu.make_async_copy(gram_ref, gram, small.at[0])
+    load.start()
+    for i in range(8):
+        copies(i)[0].start()
+    for i in range(4):
+        copies(i)[0].wait()
+        copies(i)[1].start()
+    load.wait()
+    first = lax.axis_index("orb") < NX4
+    scale = 1.0 / (ROWS * NZ * NDOM)
+    stores = []
+    for m, ref in enumerate((h_ref, s_ref)):
+        own, across = gram[2 * m] * scale, gram[2 * m + 1] * scale
+        low = jnp.where(first, own, across)
+        high = jnp.where(first, across, own)
+        pair[m] = jnp.concatenate([low[:, :W], high[:, :W]], 1)
+        stores.append(pltpu.make_async_copy(pair.at[m], ref, small.at[1 + m]))
+        stores[m].start()
+    for i in range(4, 8):
+        copies(i)[0].wait()
+        copies(i)[1].start()
+    for i in range(8):
+        copies(i)[1].wait()
+    for c in stores:
+        c.wait()
 
 
 def on_device(orbitals, potential, proj_index, proj_values, proj_energy):
@@ -583,16 +622,25 @@
         wz,
         cy,
     )
-    first = lax.axis_index("orb") < NX4
-    cells = ROWS * NZ * lax.axis_size("dom")
-
-    def whole(own, across):
-        own, across = own[:, :W], across[:, :W]
-        low = jnp.where(first, own, across)
-        high = jnp.where(first, across, own)
-        return jnp.concatenate([low, high], 1) / cells
-
-    return filtered.reshape(orbitals.shape), whole(gram[0], gram[1]), whole(gram[2], gram[3])
+    filtered, ham, corr = pl.pallas_call(
+        finish,
+        out_shape=(
+            jax.ShapeDtypeStruct((ORB, ROWS, NZ), F32),
+            jax.ShapeDtypeStruct((ORB, 2 * W), F32),
+            jax.ShapeDtypeStruct((ORB, 2 * W), F32),
+        ),
+        in_specs=[hbm, hbm],
+        out_specs=(hbm, hbm, hbm),
+        scratch_shapes=[
+            pltpu.VMEM((ORB, ROWS, NZ), F32),
+            pltpu.VMEM((4, ORB, 128), F32),
+            pltpu.VMEM((2, ORB, 2 * W), F32),
+            dma((2, 8)),
+            dma((3,)),
+        ],
+        name="outputs",
+    )(filtered, gram)
+    return filtered.reshape(orbitals.shape), ham, corr
 
 
 def solution(mesh):

time: 132 us -> 113 us (0.86)
  Pallas kernels: 125 us -> 112 us
  local copies, waits for them, and re-layouts: 4.06 us -> 0 us
  other arithmetic: 1.38 us -> 0 us
    pallas_call x1, Pallas kernels: 125 us -> 109 us  [on_device(): pl.pallas_call(kernel, out_shape=(jax.ShapeDtypeStruct((ORB, ROWS, NZ), F...]
    unnamed x1 -> x0, local copies, waits for them, and re-layouts: 3.3 us -> none
    pallas_call x0 -> x1, Pallas kernels: none -> 2.69 us  [on_device(): pl.pallas_call(finish, out_shape=(jax.ShapeDtypeStruct((ORB, ROWS, NZ), F...]
    div x2 -> x0, other arithmetic: 1.37 us -> none  [whole(): return jnp.concatenate([low, high], 1) / cells]
where the time goes in v2:
time: 113 us; the launch traced here: 112 us
  Pallas kernels  112 us (99%)
    pallas_call x1, Pallas kernels, on_device(): pl.pallas_call(kernel, out_shape=(jax.ShapeDtypeStruct((ORB, ROWS, NZ), F...  109 us
    pallas_call x1, Pallas kernels, on_device(): pl.pallas_call(finish, out_shape=(jax.ShapeDtypeStruct((ORB, ROWS, NZ), F...  2.69 us

profile of v2, /device:TPU:1, one launch (start us, length us, event | category | flops | bytes accessed | tf_op | source)
XLA Modules:
  0.0 112.4 jit_solution(1480241560892054838)
XLA Ops:
  0.6 109.0 %filter_step.1 = (f32[24,192,128]{2,1,0:T(8,128)}, f32[4,24,128]{2,1,0:T(8,128)}) custom-call(f32[24,192,128]{2,1,0:T(8,128)} %bitcast.4, f32[192,128]{1,0:T(8,128)} %bitcast.5, s32[64,96]{1,0:T(8,128)} %idx_ref.1, f32[64,96]{1,0:T(8,128)} %val_ref.1, f32[1,64]{1,0:T(1,128)} %bitcast.6, bf16[256,256]{1,0:T(8,128)(2,1)} %constant.18.wz_ref, ...), custom_call_target="tpu_custom_call" | custom-call | tf_op jit(solution)/shard_map/filter_step/pallas_call | solution.py:568
  109.7 2.7 %outputs.1 = (f32[24,192,128]{2,1,0:T(8,128)}, f32[24,192]{1,0:T(8,128)}, f32[24,192]{1,0:T(8,128)}) custom-call(f32[24,192,128]{2,1,0:T(8,128)} %get-tuple-element.8.full_ref, f32[4,24,128]{2,1,0:T(8,128)} %get-tuple-element.9.gram_ref), custom_call_target="tpu_custom_call" | custom-call | tf_op jit(solution)/shard_map/outputs/pallas_call | solution.py:625

commit v3 on v2

--- a/solution.py
+++ b/solution.py
@@ -406,9 +406,35 @@
         return g[:, :128] + g[:, 128:]
 
     def put(m, h, g):
-        snd_own[:, 2 * m + h] = g[:W].reshape(NX4, ORB, 128)
+        snd_own[m, :, h] = g[:W].reshape(NX4, ORB, 128)
         if h:
-            snd_x[:, m] = jnp.transpose(g)[:W].reshape(NX4, ORB, 128)
+            snd_x[m] = jnp.transpose(g)[:W].reshape(NX4, ORB, 128)
+
+    def rows_own(m, k):
+        to = (dom, row * NX4 + xpeer(k))
+        return remote(snd_own.at[m, xpeer(k)], rcv_own.at[m, k], r1s.at[m, k], r1r.at[m, k], to)
+
+    def rows_x(m, k):
+        to = (dom, other + xpeer(k))
+        return remote(snd_x.at[m, xpeer(k)], rcv_x.at[m, k], r1s.at[m, 4 + k], r1r.at[m, 4 + k], to)
+
+    def send_rows(m):
+        for k in range(4):
+            rows_x(m, k).start()
+        for k in range(1, 4):
+            rows_own(m, k).start()
+
+    def add_rows(m):
+        own = snd_own[m, xx]
+        for k in range(1, 4):
+            rows_own(m, k).wait_recv()
+            own = own + rcv_own[m, k]
+        cr = own[1]
+        for k in range(4):
+            rows_x(m, k).wait_recv()
+            cr = cr + rcv_x[m, k]
+        red[2 * m] = own[0]
+        red[2 * m + 1] = cr
 
     split(fa, XR, fb, 0, XR)
     put(1, 0, mul(fb[...], fb[...]))
@@ -425,6 +451,7 @@
         put(1, 1, mul(fb[:, XA * NZ :], ob[:, : XB * NZ]))
 
     by_row(across_zero, across_one)
+    send_rows(1)
 
     def image_zero():
         put(0, 1, mul(ib[:, : XA * NZ], ob[...]))
@@ -439,32 +466,9 @@
         put(0, 1, mul(fb[:, XA * NZ :], ob[:, : XB * NZ]))
 
     by_row(image_zero, image_one)
-
-    def rows_own(k):
-        return remote(
-            snd_own.at[xpeer(k)], rcv_own.at[k], r1s.at[k], r1r.at[k], (dom, row * NX4 + xpeer(k))
-        )
-
-    def rows_x(k):
-        return remote(
-            snd_x.at[xpeer(k)], rcv_x.at[k], r1s.at[4 + k], r1r.at[4 + k], (dom, other + xpeer(k))
-        )
-
-    for k in range(4):
-        rows_x(k).start()
-    for k in range(1, 4):
-        rows_own(k).start()
-    total = snd_own[xx]
-    for k in range(1, 4):
-        rows_own(k).wait_recv()
-        total = total + rcv_own[k]
-    cr = jnp.zeros((2, ORB, 128), F32)
-    for k in range(4):
-        rows_x(k).wait_recv()
-        cr = cr + rcv_x[k]
-    red[...] = total
-    red[1] = total[1] + cr[0]
-    red[3] = total[3] + cr[1]
+    send_rows(0)
+    add_rows(1)
+    add_rows(0)
 
     def quarter(k):
         t = lax.rem(tt + k, 4)
@@ -509,12 +513,14 @@
             by_row(lambda: cross_image(q, k).wait_send(), None)
 
     loop(NQ, sent)
+    for m in range(2):
+        for k in range(1, 4):
+            rows_own(m, k).wait_send()
+        for k in range(4):
+            rows_x(m, k).wait_send()
     for k in range(1, 4):
-        rows_own(k).wait_send()
         quarter(k).wait_send()
         back(k).wait_send()
-    for k in range(4):
-        rows_x(k).wait_send()
     for k in range(1, 8):
         along(k).wait_send()
     for k in range(1, 4):
@@ -590,10 +596,10 @@
             pltpu.VMEM((256, K), BF16),
             pltpu.VMEM((256, K), BF16),
             pltpu.VMEM((256, XA * NZ), BF16),
-            pltpu.VMEM((NX4, 4, ORB, 128), F32),
-            pltpu.VMEM((NX4, 2, ORB, 128), F32),
-            pltpu.VMEM((NX4, 4, ORB, 128), F32),
-            pltpu.VMEM((NX4, 2, ORB, 128), F32),
+            pltpu.VMEM((2, NX4, 2, ORB, 128), F32),
+            pltpu.VMEM((2, NX4, ORB, 128), F32),
+            pltpu.VMEM((2, NX4, 2, ORB, 128), F32),
+            pltpu.VMEM((2, NX4, ORB, 128), F32),
             pltpu.VMEM((4, ORB, 128), F32),
             pltpu.VMEM((4, ORB, 128), F32),
             pltpu.VMEM((8, ORB, 128), F32),
@@ -604,7 +610,7 @@
             dma((NQ, 4)), dma((NQ, 4)),
             dma((NQ, 4)), dma((NQ, 4)),
             dma((NQ, 4)), dma((NQ, 4)),
-            dma((8,)), dma((8,)),
+            dma((2, 8)), dma((2, 8)),
             dma((4,)), dma((4,)),
             dma((8,)), dma((8,)),
             dma((4,)), dma((4,)),

time: 113 us -> 112 us (level)
  no operation moved by 1% of the time
where the time goes in v3:
time: 112 us
  Pallas kernels  111 us (99%)
    pallas_call x1, Pallas kernels, on_device(): pl.pallas_call(kernel, out_shape=(jax.ShapeDtypeStruct((ORB, ROWS, NZ), F...  108 us
    pallas_call x1, Pallas kernels, on_device(): pl.pallas_call(finish, out_shape=(jax.ShapeDtypeStruct((ORB, ROWS, NZ), F...  2.69 us

profile of v3, /device:TPU:1, one launch (start us, length us, event | category | flops | bytes accessed | tf_op | source)
XLA Modules:
  0.0 111.8 jit_solution(3154036260574053879)
XLA Ops:
  0.6 108.5 %filter_step.1 = (f32[24,192,128]{2,1,0:T(8,128)}, f32[4,24,128]{2,1,0:T(8,128)}) custom-call(f32[24,192,128]{2,1,0:T(8,128)} %bitcast.4, f32[192,128]{1,0:T(8,128)} %bitcast.5, s32[64,96]{1,0:T(8,128)} %idx_ref.1, f32[64,96]{1,0:T(8,128)} %val_ref.1, f32[1,64]{1,0:T(1,128)} %bitcast.6, bf16[256,256]{1,0:T(8,128)(2,1)} %constant.18.wz_ref, ...), custom_call_target="tpu_custom_call" | custom-call | tf_op jit(solution)/shard_map/filter_step/pallas_call | solution.py:574
  109.1 2.7 %outputs.1 = (f32[24,192,128]{2,1,0:T(8,128)}, f32[24,192]{1,0:T(8,128)}, f32[24,192]{1,0:T(8,128)}) custom-call(f32[24,192,128]{2,1,0:T(8,128)} %get-tuple-element.8.full_ref, f32[4,24,128]{2,1,0:T(8,128)} %get-tuple-element.9.gram_ref), custom_call_target="tpu_custom_call" | custom-call | tf_op jit(solution)/shard_map/outputs/pallas_call | solution.py:631
